TPU v7x, 32 devices: a whole 2x2x4 slice. The times are simulated.
32 devices in a mesh: ctx: 4 (over x, core), fsdp: 8 (over z, y).
Axes of the slice: x: 2, y: 2, z: 4, core: 2. Of those that a mesh axis runs over, the one named last changes fastest.
Arguments:
- tokens: bfloat16 [8, 4, 2, 448, 576], P('fsdp', 'ctx'), may hold values from -6 to 6
- positions: int32 [8, 4, 2, 448], P('fsdp', 'ctx'), may hold values from 0 to 3583, as said below
- attn_gain: bfloat16 [576], P('fsdp'), may hold values from 0.099609375 to 1.8984375
- w_query: bfloat16 [576, 576], P('fsdp'), may hold values from -0.25 to 0.25
- w_key: bfloat16 [576, 192], P('fsdp'), may hold values from -0.25 to 0.25
- w_value: bfloat16 [576, 192], P('fsdp'), may hold values from -0.25 to 0.25
- w_out: bfloat16 [576, 576], P('fsdp'), may hold values from -4 to 4
- mlp_gain: bfloat16 [576], P('fsdp'), may hold values from 0.099609375 to 1.8984375
- w_gate: bfloat16 [576, 1536], P('fsdp'), may hold values from -0.25 to 0.25
- w_up: bfloat16 [576, 1536], P('fsdp'), may hold values from -0.25 to 0.25
- w_down: bfloat16 [1536, 576], P('fsdp'), may hold values from -0.15625 to 0.15625
- cotangent: bfloat16 [8, 4, 2, 448, 576], P('fsdp', 'ctx'), may hold values from -6 to 6
Outputs:
- block_out: float32 [8, 4, 2, 448, 576], P('fsdp', 'ctx')
- tokens_grad: float32 [8, 4, 2, 448, 576], P('fsdp', 'ctx')
- attn_gain_grad: float32 [576], P('fsdp')
- query_grad: float32 [576, 576], P('fsdp')
- key_grad: float32 [576, 192], P('fsdp')
- value_grad: float32 [576, 192], P('fsdp')
- out_grad: float32 [576, 576], P('fsdp')
- mlp_gain_grad: float32 [576], P('fsdp')
- gate_grad: float32 [576, 1536], P('fsdp')
- up_grad: float32 [576, 1536], P('fsdp')
- down_grad: float32 [1536, 576], P('fsdp')
Inputs may be any that keep to these rules, and one draw needn't show every extreme that they name: `positions`: each sequence is a pack of documents: a token's position counts the tokens before it in its own document, in natural order, and is 0 at each document's first token and at the sequence's first token; at least one sequence of each draw is a single document.
All inputs are finite; a program needn't handle non-finite values.
Results may differ from a plain program's by a relative error of at most 0.02.
Values may be sent and summed in bfloat16 or wider, within the bound.
A program may use at most 384 MiB of HBM per device.

v0:
```python
import jax
import jax.numpy as jnp
from jax import lax
from jax.sharding import PartitionSpec as P

HD = 64


NORM_EPS = 1e-05
ROPE_BASE = 100000.0
ATTN_SCALE = 0.125
MASKED = -1e30


def rope_tables(positions):
    exponents = jnp.arange(HD // 2, dtype=jnp.float32) * (2.0 / HD)
    frequency = jnp.exp(-exponents * jnp.log(jnp.float32(ROPE_BASE)))
    angles = positions.astype(jnp.float32)[:, None] * frequency[None, :]
    return (jnp.cos(angles)[:, None, :], jnp.sin(angles)[:, None, :])


def rotate(field, cosines, sine_vals):
    front_half = field[..., : HD // 2]
    back_half = field[..., HD // 2 :]
    return jnp.concatenate(
        [
            front_half * cosines - back_half * sine_vals,
            back_half * cosines + front_half * sine_vals,
        ],
        axis=-1,
    )


def rms_scale(field):
    return lax.rsqrt(jnp.mean(field * field, axis=-1, keepdims=True) + NORM_EPS)


def natural_rows(row_ids, block_len, ctx_count):
    device_id = row_ids // (2 * block_len)
    in_pair = row_ids // block_len % 2
    within = row_ids % block_len
    block_id = jnp.where(in_pair == 0, device_id, 2 * ctx_count - 1 - device_id)
    return block_id * block_len + within


def masked_scores(query_grp, key_grp, query_nat, key_nat):
    scores = (
        jnp.einsum("qhd,kd->hqk", query_grp, key_grp, preferred_element_type=jnp.float32)
        * ATTN_SCALE
    )
    allowed = query_nat[:, None] >= key_nat[None, :]
    return jnp.where(allowed[None], scores, MASKED)


def rows_by_cols(left, right):
    return jnp.einsum("rd,rf->df", left, right, preferred_element_type=jnp.float32)


def times_transpose(left, right):
    return jnp.einsum("rf,df->rd", left, right, preferred_element_type=jnp.float32)


def local(
    tokens,
    positions,
    attn_gain,
    w_query,
    w_key,
    w_value,
    w_out,
    mlp_gain,
    w_gate,
    w_up,
    w_down,
    cotangent,
):
    seq_count = tokens.shape[0]
    block_len = tokens.shape[3]
    model_width = tokens.shape[4]
    pair_len = 2 * block_len
    row_total = seq_count * pair_len
    ctx_count = lax.axis_size("ctx")
    ctx_id = lax.axis_index("ctx")
    layer_in = tokens.reshape(row_total, model_width).astype(jnp.float32)
    cosines, sine_vals = rope_tables(positions.reshape(row_total))
    local_nat = natural_rows(
        ctx_id * pair_len + jnp.arange(pair_len, dtype=jnp.int32), block_len, ctx_count
    )
    key_nat = natural_rows(jnp.arange(pair_len * ctx_count, dtype=jnp.int32), block_len, ctx_count)
    weights_full = (
        lax.all_gather(attn_gain, "fsdp", axis=0, tiled=True),
        lax.all_gather(w_query, "fsdp", axis=0, tiled=True),
        lax.all_gather(w_key, "fsdp", axis=0, tiled=True),
        lax.all_gather(w_value, "fsdp", axis=0, tiled=True),
        lax.all_gather(w_out, "fsdp", axis=0, tiled=True),
        lax.all_gather(mlp_gain, "fsdp", axis=0, tiled=True),
        lax.all_gather(w_gate, "fsdp", axis=0, tiled=True),
        lax.all_gather(w_up, "fsdp", axis=0, tiled=True),
        lax.all_gather(w_down, "fsdp", axis=0, tiled=True),
    )
    gain_one, query_w, key_w, value_w, out_w, gain_two, gate_w, up_w, down_w = weights_full
    num_heads = query_w.shape[1] // HD
    kv_heads = key_w.shape[1] // HD
    group_size = num_heads // kv_heads
    query_width = num_heads * HD
    kv_width = kv_heads * HD
    inv_one = rms_scale(layer_in)
    normed = (layer_in * inv_one * gain_one.astype(jnp.float32)).astype(jnp.bfloat16)
    query_raw = jnp.dot(normed, query_w, preferred_element_type=jnp.float32).reshape(
        row_total, num_heads, HD
    )
    key_raw = jnp.dot(normed, key_w, preferred_element_type=jnp.float32).reshape(
        row_total, kv_heads, HD
    )
    queries = rotate(query_raw, cosines, sine_vals).astype(jnp.bfloat16)
    key_rows = rotate(key_raw, cosines, sine_vals).astype(jnp.bfloat16)
    value_rows = jnp.dot(normed, value_w, preferred_element_type=jnp.float32).astype(jnp.bfloat16)
    key_value = jnp.concatenate(
        [key_rows.reshape(row_total, kv_width), value_rows], axis=-1
    ).reshape(seq_count, pair_len, 2 * kv_width)
    query_seqs = queries.reshape(seq_count, pair_len, num_heads, HD)

    def forward_seq(carried, element):
        query_seq, kv_seq = element
        kv_all = lax.all_gather(kv_seq, "ctx", axis=0, tiled=True)
        keys_all = kv_all[:, :kv_width].reshape(-1, kv_heads, HD)
        values_all = kv_all[:, kv_width:].reshape(-1, kv_heads, HD)
        out_parts = []
        lse_parts = []
        for head_group in range(kv_heads):
            head_lo = head_group * group_size
            query_grp = query_seq[:, head_lo : head_lo + group_size]
            scores = masked_scores(query_grp, keys_all[:, head_group], local_nat, key_nat)
            row_max = jnp.max(scores, axis=-1, keepdims=True)
            exponent = jnp.exp(scores - row_max)
            row_total_exp = jnp.sum(exponent, axis=-1, keepdims=True)
            attn_probs = (exponent / row_total_exp).astype(jnp.bfloat16)
            out_parts.append(
                jnp.einsum(
                    "hqk,kd->qhd",
                    attn_probs,
                    values_all[:, head_group],
                    preferred_element_type=jnp.float32,
                )
            )
            lse_parts.append((row_max + jnp.log(row_total_exp))[:, :, 0])
        attended_seq = (
            jnp.concatenate(out_parts, axis=1).reshape(pair_len, query_width).astype(jnp.bfloat16)
        )
        log_sum = jnp.concatenate(lse_parts, axis=0).T
        return (carried, (attended_seq, log_sum))

    forward_out = lax.scan(forward_seq, None, (query_seqs, key_value))
    attended, log_sums = forward_out[1]
    attended_flat = attended.reshape(row_total, query_width)
    hidden = layer_in + jnp.dot(attended_flat, out_w, preferred_element_type=jnp.float32)
    inv_two = rms_scale(hidden)
    second = (hidden * inv_two * gain_two.astype(jnp.float32)).astype(jnp.bfloat16)
    gate_proj = jnp.dot(second, gate_w, preferred_element_type=jnp.float32)
    up_proj = jnp.dot(second, up_w, preferred_element_type=jnp.float32)
    inner_act = (jax.nn.silu(gate_proj) * up_proj).astype(jnp.bfloat16)
    block_out = hidden + jnp.dot(inner_act, down_w, preferred_element_type=jnp.float32)
    weights_back = (
        lax.all_gather(attn_gain, "fsdp", axis=0, tiled=True),
        lax.all_gather(w_query, "fsdp", axis=0, tiled=True),
        lax.all_gather(w_key, "fsdp", axis=0, tiled=True),
        lax.all_gather(w_value, "fsdp", axis=0, tiled=True),
        lax.all_gather(w_out, "fsdp", axis=0, tiled=True),
        lax.all_gather(mlp_gain, "fsdp", axis=0, tiled=True),
        lax.all_gather(w_gate, "fsdp", axis=0, tiled=True),
        lax.all_gather(w_up, "fsdp", axis=0, tiled=True),
        lax.all_gather(w_down, "fsdp", axis=0, tiled=True),
    )
    gain_one, query_w, key_w, value_w, out_w, gain_two, gate_w, up_w, down_w = weights_back
    grad_out = cotangent.reshape(row_total, model_width)
    down_wgrad = rows_by_cols(inner_act, grad_out)
    inner_grad = times_transpose(grad_out, down_w)
    sigmoid_gate = jax.nn.sigmoid(gate_proj)
    silu_val = gate_proj * sigmoid_gate
    silu_slope = sigmoid_gate * (1.0 + gate_proj * (1.0 - sigmoid_gate))
    gate_back = (inner_grad * up_proj * silu_slope).astype(jnp.bfloat16)
    up_back = (inner_grad * silu_val).astype(jnp.bfloat16)
    gate_wgrad = rows_by_cols(second, gate_back)
    up_wgrad = rows_by_cols(second, up_back)
    second_grad = times_transpose(gate_back, gate_w) + times_transpose(up_back, up_w)
    gain_two_grad = jnp.sum(second_grad * hidden * inv_two, axis=0)
    scaled_two = second_grad * gain_two.astype(jnp.float32)
    hidden_grad = (
        grad_out.astype(jnp.float32)
        + inv_two * scaled_two
        - hidden * inv_two**3 * jnp.mean(scaled_two * hidden, axis=-1, keepdims=True)
    )
    hidden_low = hidden_grad.astype(jnp.bfloat16)
    out_wgrad = rows_by_cols(attended_flat, hidden_low)
    attended_grad = (
        times_transpose(hidden_low, out_w)
        .astype(jnp.bfloat16)
        .reshape(seq_count, pair_len, num_heads, HD)
    )

    def backward_seq(carried, element):
        query_seq, kv_seq, grad_seq, lse_seq = element
        kv_all = lax.all_gather(kv_seq, "ctx", axis=0, tiled=True)
        keys_all = kv_all[:, :kv_width].reshape(-1, kv_heads, HD)
        values_all = kv_all[:, kv_width:].reshape(-1, kv_heads, HD)
        query_parts = []
        delta_parts = []
        key_parts = []
        value_parts = []
        for head_group in range(kv_heads):
            head_lo = head_group * group_size
            query_grp = query_seq[:, head_lo : head_lo + group_size]
            grad_grp = grad_seq[:, head_lo : head_lo + group_size]
            scores = masked_scores(query_grp, keys_all[:, head_group], local_nat, key_nat)
            attn_probs = jnp.exp(scores - lse_seq[:, head_lo : head_lo + group_size].T[:, :, None])
            prob_grad = jnp.einsum(
                "qhd,kd->hqk",
                grad_grp,
                values_all[:, head_group],
                preferred_element_type=jnp.float32,
            )
            delta_grp = jnp.sum(attn_probs * prob_grad, axis=-1, keepdims=True)
            score_grad = (attn_probs * (prob_grad - delta_grp)).astype(jnp.bfloat16)
            query_parts.append(
                jnp.einsum(
                    "hqk,kd->qhd",
                    score_grad,
                    keys_all[:, head_group],
                    preferred_element_type=jnp.float32,
                )
                * ATTN_SCALE
            )
            delta_parts.append(delta_grp[:, :, 0])
            key_parts.append(
                jnp.einsum("hqk,qhd->kd", score_grad, query_grp, preferred_element_type=jnp.float32)
                * ATTN_SCALE
            )
            value_parts.append(
                jnp.einsum(
                    "hqk,qhd->kd",
                    attn_probs.astype(jnp.bfloat16),
                    grad_grp,
                    preferred_element_type=jnp.float32,
                )
            )
        query_grad_seq = jnp.concatenate(query_parts, axis=1)
        kv_terms = jnp.concatenate(key_parts + value_parts, axis=-1)
        kv_grad_seq = lax.psum_scatter(kv_terms, "ctx", scatter_dimension=0, tiled=True)
        return (carried, (query_grad_seq, kv_grad_seq))

    backward_out = lax.scan(backward_seq, None, (query_seqs, key_value, attended_grad, log_sums))
    query_grad_all, kv_grad_all = backward_out[1]
    query_back = (
        rotate(query_grad_all.reshape(row_total, num_heads, HD), cosines, -sine_vals)
        .reshape(row_total, query_width)
        .astype(jnp.bfloat16)
    )
    key_back = (
        rotate(kv_grad_all[:, :, :kv_width].reshape(row_total, kv_heads, HD), cosines, -sine_vals)
        .reshape(row_total, kv_width)
        .astype(jnp.bfloat16)
    )
    value_back = kv_grad_all[:, :, kv_width:].reshape(row_total, kv_width).astype(jnp.bfloat16)
    query_wgrad = rows_by_cols(normed, query_back)
    key_wgrad = rows_by_cols(normed, key_back)
    value_wgrad = rows_by_cols(normed, value_back)
    normed_grad = (
        times_transpose(query_back, query_w)
        + times_transpose(key_back, key_w)
        + times_transpose(value_back, value_w)
    )
    gain_one_grad = jnp.sum(normed_grad * layer_in * inv_one, axis=0)
    scaled_one = normed_grad * gain_one.astype(jnp.float32)
    input_grad = (
        hidden_grad
        + inv_one * scaled_one
        - layer_in * inv_one**3 * jnp.mean(scaled_one * layer_in, axis=-1, keepdims=True)
    )
    shares = (
        lax.psum_scatter(
            gain_one_grad.astype(jnp.bfloat16), "fsdp", scatter_dimension=0, tiled=True
        ).astype(jnp.float32),
        lax.psum_scatter(
            query_wgrad.astype(jnp.bfloat16), "fsdp", scatter_dimension=0, tiled=True
        ).astype(jnp.float32),
        lax.psum_scatter(
            key_wgrad.astype(jnp.bfloat16), "fsdp", scatter_dimension=0, tiled=True
        ).astype(jnp.float32),
        lax.psum_scatter(
            value_wgrad.astype(jnp.bfloat16), "fsdp", scatter_dimension=0, tiled=True
        ).astype(jnp.float32),
        lax.psum_scatter(
            out_wgrad.astype(jnp.bfloat16), "fsdp", scatter_dimension=0, tiled=True
        ).astype(jnp.float32),
        lax.psum_scatter(
            gain_two_grad.astype(jnp.bfloat16), "fsdp", scatter_dimension=0, tiled=True
        ).astype(jnp.float32),
        lax.psum_scatter(
            gate_wgrad.astype(jnp.bfloat16), "fsdp", scatter_dimension=0, tiled=True
        ).astype(jnp.float32),
        lax.psum_scatter(
            up_wgrad.astype(jnp.bfloat16), "fsdp", scatter_dimension=0, tiled=True
        ).astype(jnp.float32),
        lax.psum_scatter(
            down_wgrad.astype(jnp.bfloat16), "fsdp", scatter_dimension=0, tiled=True
        ).astype(jnp.float32),
    )
    totals = (
        lax.psum(shares[0].astype(jnp.bfloat16), "ctx").astype(jnp.float32),
        lax.psum(shares[1].astype(jnp.bfloat16), "ctx").astype(jnp.float32),
        lax.psum(shares[2].astype(jnp.bfloat16), "ctx").astype(jnp.float32),
        lax.psum(shares[3].astype(jnp.bfloat16), "ctx").astype(jnp.float32),
        lax.psum(shares[4].astype(jnp.bfloat16), "ctx").astype(jnp.float32),
        lax.psum(shares[5].astype(jnp.bfloat16), "ctx").astype(jnp.float32),
        lax.psum(shares[6].astype(jnp.bfloat16), "ctx").astype(jnp.float32),
        lax.psum(shares[7].astype(jnp.bfloat16), "ctx").astype(jnp.float32),
        lax.psum(shares[8].astype(jnp.bfloat16), "ctx").astype(jnp.float32),
    )
    return (
        block_out.reshape(tokens.shape),
        input_grad.reshape(tokens.shape),
        totals[0],
        totals[1],
        totals[2],
        totals[3],
        totals[4],
        totals[5],
        totals[6],
        totals[7],
        totals[8],
    )


def solution(mesh):
    placed = (
        P("fsdp", "ctx", None, None, None),
        P("fsdp", "ctx", None, None),
        P("fsdp"),
        P("fsdp", None),
        P("fsdp", None),
        P("fsdp", None),
        P("fsdp", None),
        P("fsdp"),
        P("fsdp", None),
        P("fsdp", None),
        P("fsdp", None),
        P("fsdp", "ctx", None, None, None),
    )
    return jax.shard_map(
        local,
        mesh=mesh,
        in_specs=placed,
        out_specs=(
            P("fsdp", "ctx", None, None, None),
            P("fsdp", "ctx", None, None, None),
            P("fsdp"),
            P("fsdp", None),
            P("fsdp", None),
            P("fsdp", None),
            P("fsdp", None),
            P("fsdp"),
            P("fsdp", None),
            P("fsdp", None),
            P("fsdp", None),
        ),
        check_vma=False,
    )
```

profile of v0, /device:TPU:0, one launch (start us, length us, event | category | flops | bytes accessed | tf_op | source)
XLA Modules:
  0.0 1087.8 jit_solution(138087373751630101)
XLA Ops:
  11.0 23.1 %all-reduce.7 = (bf16[576]{0:T(1024)(128)(2,1)S(1)}, bf16[576]{0:T(1024)(128)(2,1)S(1)}) all-reduce(bf16[576]{0:T(1024)(128)(2,1)S(1)} %dynamic-update-slice, bf16[576]{0:T(1024)(128)(2,1)S(1)} %dynamic-update-slice.1), channel_id=1, replica_groups=mesh['ctx'=4,'fsdp'=8] {'fsdp'}, use_global_device_ids=true, to_apply=%add | all-reduce | flops 1152 | bytes 4608
  36.5 31.0 %all_gather.43 = bf16[576,192]{1,0:T(8,128)(2,1)S(1)} all-gather(bf16[72,192]{1,0:T(8,128)(2,1)} %param.16), channel_id=1, replica_groups=mesh['ctx'=4,'fsdp'=8] {'fsdp'}, dimensions={0}, use_global_device_ids=true | all-gather | bytes 248832 | tf_op jit(solution)/shard_map/all_gather | solution.py:93
  68.4 33.2 %all_gather.44 = bf16[576,192]{1,0:T(8,128)(2,1)} all-gather(bf16[72,192]{1,0:T(8,128)(2,1)} %param.17), channel_id=1, replica_groups=mesh['ctx'=4,'fsdp'=8] {'fsdp'}, dimensions={0}, use_global_device_ids=true | all-gather | bytes 248832 | tf_op jit(solution)/shard_map/all_gather | solution.py:94
  111.6 32.4 %all_gather.46 = bf16[576,576]{1,0:T(8,128)(2,1)S(1)} all-gather(bf16[72,576]{1,0:T(8,128)(2,1)S(1)} %copy-done.41), channel_id=1, replica_groups=mesh['ctx'=4,'fsdp'=8] {'fsdp'}, dimensions={0}, use_global_device_ids=true | all-gather | bytes 746496 | tf_op jit(solution)/shard_map/all_gather | solution.py:92
  144.0 35.4 %all_gather.47 = bf16[576,576]{1,0:T(8,128)(2,1)} all-gather(bf16[72,576]{1,0:T(8,128)(2,1)} %param.18), channel_id=1, replica_groups=mesh['ctx'=4,'fsdp'=8] {'fsdp'}, dimensions={0}, use_global_device_ids=true | all-gather | bytes 746496 | tf_op jit(solution)/shard_map/all_gather | solution.py:95
  188.9 18.4 %fusion.110 = (f32[3,896]{1,0:T(4,128)S(1)}, f32[3,896,3584]{1,2,0:T(8,128)}) fusion(bf16[896,9,32]{0,2,1:T(8,128)(2,1)S(1)} %get-tuple-element.94, bf16[896,9,32]{0,2,1:T(8,128)(2,1)S(1)} %get-tuple-element.95, bf16[3584,3,64]{0,2,1:T(8,128)(2,1)S(1)} %bitcast.205, pred[896,3584]{0,1:T(8,128)(4,1)} %broadcast_compare_fusion), kind=kOutput, calls=%fused_computation.205 | convolution fusion | flops 1262712192 | bytes 43248128 | tf_op jit(solution)/shard_map/while/body/eval_jaxpr/qhd,kd->hqk/dot_general | solution.py:48
  207.2 17.6 %fusion.109 = (f32[3,896]{1,0:T(4,128)S(1)}, f32[3,896,3584]{1,2,0:T(8,128)}) fusion(bf16[896,9,32]{0,2,1:T(8,128)(2,1)S(1)} %get-tuple-element.95, bf16[896,9,32]{0,2,1:T(8,128)(2,1)S(1)} %get-tuple-element.94, bf16[3584,3,64]{0,2,1:T(8,128)(2,1)S(1)} %bitcast.206, pred[896,3584]{0,1:T(8,128)(4,1)} %broadcast_compare_fusion), kind=kOutput, calls=%fused_computation.204 | convolution fusion | flops 1262712192 | bytes 43248128 | tf_op jit(solution)/shard_map/while/body/eval_jaxpr/qhd,kd->hqk/dot_general | solution.py:48
  224.9 17.7 %fusion.111 = (f32[3,896]{1,0:T(4,128)S(1)}, f32[3,896,3584]{1,2,0:T(8,128)}) fusion(bf16[896,9,32]{0,2,1:T(8,128)(2,1)S(1)} %get-tuple-element.94, bf16[896,9,32]{0,2,1:T(8,128)(2,1)S(1)} %get-tuple-element.95, bf16[3584,3,64]{0,2,1:T(8,128)(2,1)S(1)} %bitcast.207, pred[896,3584]{0,1:T(8,128)(4,1)} %broadcast_compare_fusion), kind=kOutput, calls=%fused_computation.206 | convolution fusion | flops 1262712192 | bytes 43248128 | tf_op jit(solution)/shard_map/while/body/eval_jaxpr/qhd,kd->hqk/dot_general | solution.py:48
  242.6 15.1 %fusion.10 = f32[3,896]{1,0:T(4,128)S(1)} fusion(f32[3,896,3584]{1,2,0:T(8,128)} %get-tuple-element.113, f32[3,896]{1,0:T(4,128)S(1)} %get-tuple-element.112), kind=kLoop, calls=%fused_computation.28 | loop fusion | flops 19264896 | bytes 38556672 | tf_op jit(solution)/shard_map/while/body/eval_jaxpr/reduce_sum | solution.py:136
  257.7 14.5 %fusion.59 = bf16[896,3,64]{0,2,1:T(8,128)(2,1)S(1)} fusion(f32[3,896,3584]{1,2,0:T(8,128)} %get-tuple-element.113, f32[3,896]{1,0:T(4,128)S(1)} %fusion.10, f32[3,896]{1,0:T(4,128)S(1)} %get-tuple-element.112, bf16[3584,3,64]{0,2,1:T(8,128)(2,1)S(1)} %bitcast.211), kind=kOutput, calls=%fused_computation.99 | convolution fusion | flops 1262198784 | bytes 39366656 | tf_op jit(solution)/shard_map/while/body/eval_jaxpr/hqk,kd->qhd/dot_general | solution.py:139
  272.2 15.1 %fusion.11 = f32[3,896]{1,0:T(4,128)S(1)} fusion(f32[3,896,3584]{1,2,0:T(8,128)} %get-tuple-element.111, f32[3,896]{1,0:T(4,128)S(1)} %get-tuple-element.110), kind=kLoop, calls=%fused_computation.29 | loop fusion | flops 19264896 | bytes 38556672 | tf_op jit(solution)/shard_map/while/body/eval_jaxpr/reduce_sum | solution.py:136
  287.3 14.2 %fusion.60 = bf16[896,3,64]{0,2,1:T(8,128)(2,1)S(1)} fusion(f32[3,896,3584]{1,2,0:T(8,128)} %get-tuple-element.111, f32[3,896]{1,0:T(4,128)S(1)} %fusion.11, f32[3,896]{1,0:T(4,128)S(1)} %get-tuple-element.110, bf16[3584,3,64]{0,2,1:T(8,128)(2,1)S(1)} %bitcast.212), kind=kOutput, calls=%fused_computation.100 | convolution fusion | flops 1262198784 | bytes 39366656 | tf_op jit(solution)/shard_map/while/body/eval_jaxpr/hqk,kd->qhd/dot_general | solution.py:139
  301.5 15.1 %fusion.9 = f32[3,896]{1,0:T(4,128)S(1)} fusion(f32[3,896,3584]{1,2,0:T(8,128)} %get-tuple-element.115, f32[3,896]{1,0:T(4,128)S(1)} %get-tuple-element.114), kind=kLoop, calls=%fused_computation.27 | loop fusion | flops 19264896 | bytes 38556672 | tf_op jit(solution)/shard_map/while/body/eval_jaxpr/reduce_sum | solution.py:136
  316.5 14.4 %fusion.58 = bf16[896,3,64]{0,2,1:T(8,128)(2,1)S(1)} fusion(f32[3,896,3584]{1,2,0:T(8,128)} %get-tuple-element.115, f32[3,896]{1,0:T(4,128)S(1)} %fusion.9, f32[3,896]{1,0:T(4,128)S(1)} %get-tuple-element.114, bf16[3584,3,64]{0,2,1:T(8,128)(2,1)S(1)} %bitcast.213), kind=kOutput, calls=%fused_computation.98 | convolution fusion | flops 1262198784 | bytes 39366656 | tf_op jit(solution)/shard_map/while/body/eval_jaxpr/hqk,kd->qhd/dot_general | solution.py:139
  370.6 28.8 %fusion = (f32[3,896]{1,0:T(4,128)S(1)}, f32[3584,896,3]{1,0,2:T(8,128)}) fusion(f32[3,896,3584]{1,2,0:T(8,128)} %get-tuple-element.111, f32[3,896]{1,0:T(4,128)S(1)} %get-tuple-element.100, bf16[896,9,64]{0,2,1:T(8,128)(2,1)S(1)} %bitcast.221, bf16[3584,3,64]{0,2,1:T(8,128)(2,1)S(1)} %bitcast.214), kind=kOutput, calls=%fused_computation.2 | convolution fusion | flops 1262024064 | bytes 77898240 | tf_op jit(solution)/shard_map/while/body/eval_jaxpr/qhd,kd->hqk/dot_general | solution.py:216
  399.5 31.8 %fusion.2 = bf16[3,896,3584]{1,2,0:T(8,128)(2,1)} fusion(f32[3584,896,3]{1,0,2:T(8,128)} %get-tuple-element.124, f32[3,896,3584]{1,2,0:T(8,128)} %get-tuple-element.111, f32[3,896]{1,0:T(4,128)S(1)} %get-tuple-element.123, f32[3,896]{1,0:T(4,128)S(1)} %get-tuple-element.100), kind=kLoop, calls=%fused_computation.4 | loop fusion | flops 38535168 | bytes 96359424 | tf_op jit(solution)/shard_map/while/body/eval_jaxpr/convert_element_type | solution.py:223
  441.2 28.6 %fusion.3 = (f32[3,896]{1,0:T(4,128)S(1)}, f32[3584,896,3]{1,0,2:T(8,128)}) fusion(f32[3,896,3584]{1,2,0:T(8,128)} %get-tuple-element.113, f32[3,896]{1,0:T(4,128)S(1)} %get-tuple-element.101, bf16[896,9,64]{0,2,1:T(8,128)(2,1)} %bitcast.222, bf16[3584,3,64]{0,2,1:T(8,128)(2,1)} %bitcast.215), kind=kOutput, calls=%fused_computation.7 | convolution fusion | flops 1262024064 | bytes 77894656 | tf_op jit(solution)/shard_map/while/body/eval_jaxpr/qhd,kd->hqk/dot_general | solution.py:216
  469.8 31.6 %fusion.5 = bf16[3,896,3584]{1,2,0:T(8,128)(2,1)} fusion(f32[3584,896,3]{1,0,2:T(8,128)} %get-tuple-element.122, f32[3,896,3584]{1,2,0:T(8,128)} %get-tuple-element.113, f32[3,896]{1,0:T(4,128)S(1)} %get-tuple-element.121, f32[3,896]{1,0:T(4,128)S(1)} %get-tuple-element.101), kind=kLoop, calls=%fused_computation.9 | loop fusion | flops 38535168 | bytes 96359424 | tf_op jit(solution)/shard_map/while/body/eval_jaxpr/convert_element_type | solution.py:223
  511.3 28.7 %fusion.6 = (f32[3,896]{1,0:T(4,128)S(1)}, f32[3584,896,3]{1,0,2:T(8,128)}) fusion(f32[3,896,3584]{1,2,0:T(8,128)} %get-tuple-element.115, f32[3,896]{1,0:T(4,128)S(1)} %get-tuple-element.102, bf16[896,9,64]{0,2,1:T(8,128)(2,1)} %bitcast.223, bf16[3584,3,64]{0,2,1:T(8,128)(2,1)} %bitcast.216), kind=kOutput, calls=%fused_computation.12 | convolution fusion | flops 1262024064 | bytes 77894656 | tf_op jit(solution)/shard_map/while/body/eval_jaxpr/qhd,kd->hqk/dot_general | solution.py:216
  540.0 31.5 %fusion.8 = bf16[3,896,3584]{1,2,0:T(8,128)(2,1)} fusion(f32[3584,896,3]{1,0,2:T(8,128)} %get-tuple-element.120, f32[3,896,3584]{1,2,0:T(8,128)} %get-tuple-element.115, f32[3,896]{1,0:T(4,128)S(1)} %get-tuple-element.119, f32[3,896]{1,0:T(4,128)S(1)} %get-tuple-element.102), kind=kLoop, calls=%fused_computation.14 | loop fusion | flops 38535168 | bytes 96359424 | tf_op jit(solution)/shard_map/while/body/eval_jaxpr/convert_element_type | solution.py:223
  602.5 13.6 %fusion.47 = f32[3584,384]{0,1:T(8,128)} fusion(bf16[3,896,3584]{1,2,0:T(8,128)(2,1)} %fusion.8, bf16[896,9,32]{0,2,1:T(8,128)(2,1)S(1)} %copy-done.9, bf16[896,9,32]{0,2,1:T(8,128)(2,1)S(1)} %copy-done.11), kind=kOutput, calls=%fused_computation.58 | convolution fusion | flops 1234042880 | bytes 21217280 | tf_op jit(solution)/shard_map/while/body/eval_jaxpr/hqk,qhd->kd/dot_general | solution.py:235
  616.0 13.6 %fusion.49 = f32[3584,384]{0,1:T(8,128)} fusion(f32[3584,384]{0,1:T(8,128)} %fusion.47, bf16[3,896,3584]{1,2,0:T(8,128)(2,1)} %fusion.5, bf16[896,9,32]{0,2,1:T(8,128)(2,1)S(1)} %copy-done.9, bf16[896,9,32]{0,2,1:T(8,128)(2,1)S(1)} %copy-done.11), kind=kOutput, calls=%fused_computation.60 | convolution fusion | flops 1234042880 | bytes 21217280 | tf_op jit(solution)/shard_map/while/body/eval_jaxpr/hqk,qhd->kd/dot_general | solution.py:235
  636.9 15.3 %fusion.31 = f32[3584,384]{0,1:T(8,128)} fusion(f32[3584,384]{0,1:T(8,128)} %fusion.51, f32[3,896,3584]{1,2,0:T(8,128)} %get-tuple-element.115, f32[3,896]{1,0:T(4,128)S(1)} %get-tuple-element.102, bf16[896,9,64]{0,2,1:T(8,128)(2,1)S(1)} %bitcast.224), kind=kOutput, calls=%fused_computation.49 | convolution fusion | flops 1252392960 | bytes 39811072 | tf_op jit(solution)/shard_map/while/body/eval_jaxpr/hqk,qhd->kd/dot_general | solution.py:239
  652.2 15.6 %fusion.37 = f32[3584,384]{0,1:T(8,128)} fusion(f32[3584,384]{0,1:T(8,128)} %fusion.31, f32[3,896,3584]{1,2,0:T(8,128)} %get-tuple-element.113, f32[3,896]{1,0:T(4,128)S(1)} %get-tuple-element.101, bf16[896,9,64]{0,2,1:T(8,128)(2,1)S(1)} %bitcast.225), kind=kOutput, calls=%fused_computation.51 | convolution fusion | flops 1252392960 | bytes 39811072 | tf_op jit(solution)/shard_map/while/body/eval_jaxpr/hqk,qhd->kd/dot_general | solution.py:239
  667.8 45.5 %reduce-scatter.23.cloned.1.call-done = bf16[192,576]{1,0:T(8,128)(2,1)} async-done(((bf16[1536,576]{1,0:T(8,128)(2,1)}), bf16[192,576]{1,0:T(8,128)(2,1)}) %reduce-scatter.23.cloned.1.call-update) | async-done | bytes 221200 | tf_op jit(solution)/shard_map/reduce_scatter | solution.py:304
  713.3 68.8 %reduce-scatter.19.cloned.1.call-done = bf16[72,1536]{1,0:T(8,128)(2,1)} async-done(((bf16[576,1536]{1,0:T(8,128)(2,1)}), bf16[72,1536]{1,0:T(8,128)(2,1)}) %reduce-scatter.19.cloned.1.call-update) | async-done | bytes 221200 | tf_op jit(solution)/shard_map/reduce_scatter | solution.py:298
  782.1 68.3 %reduce-scatter.21.cloned.1.call-done = bf16[72,1536]{1,0:T(8,128)(2,1)} async-done(((bf16[576,1536]{1,0:T(8,128)(2,1)}), bf16[72,1536]{1,0:T(8,128)(2,1)}) %reduce-scatter.21.cloned.1.call-update) | async-done | bytes 221200 | tf_op jit(solution)/shard_map/reduce_scatter | solution.py:301
  850.4 15.5 %fusion.43 = f32[3584,384]{0,1:T(8,128)} fusion(f32[3584,384]{0,1:T(8,128)} %fusion.37, f32[3,896,3584]{1,2,0:T(8,128)} %get-tuple-element.111, f32[3,896]{1,0:T(4,128)S(1)} %copy-done.36, bf16[896,9,64]{0,2,1:T(8,128)(2,1)S(1)} %bitcast.226), kind=kOutput, calls=%fused_computation.53 | convolution fusion | flops 1252392960 | bytes 39811072 | tf_op jit(solution)/shard_map/while/body/eval_jaxpr/hqk,qhd->kd/dot_general | solution.py:239
  895.8 47.8 %reduce-scatter.13.cloned.1.call-done = f32[896,384]{0,1:T(8,128)} async-done(((f32[3584,384]{0,1:T(8,128)}), f32[896,384]{0,1:T(8,128)}) %reduce-scatter.13.cloned.1.call-update) | async-done | bytes 1376272 | tf_op jit(solution)/shard_map/while/body/eval_jaxpr/reduce_scatter | solution.py:248
  958.6 21.4 %all-reduce.6 = (bf16[576]{0:T(1024)(128)(2,1)S(1)}, bf16[576]{0:T(1024)(128)(2,1)S(1)}) all-reduce(bf16[576]{0:T(1024)(128)(2,1)S(1)} %get-tuple-element.72, bf16[576]{0:T(1024)(128)(2,1)S(1)} %copy-done.43), channel_id=3, replica_groups=mesh['ctx'=4,'fsdp'=8] {'fsdp'}, use_global_device_ids=true, to_apply=%region_15.16.clone | all-reduce | flops 1152 | bytes 4608
  987.2 18.9 %reduce-scatter.17.cloned.1.call-done = bf16[72,192]{1,0:T(8,128)(2,1)} async-done(((bf16[576,192]{1,0:T(8,128)(2,1)}), bf16[72,192]{1,0:T(8,128)(2,1)}) %reduce-scatter.17.cloned.1.call-update) | async-done | bytes 27664 | tf_op jit(solution)/shard_map/reduce_scatter | solution.py:289
  1006.1 61.0 %reduce-scatter.15.cloned.1.call-done = bf16[72,192]{1,0:T(8,128)(2,1)} async-done(((bf16[576,192]{1,0:T(8,128)(2,1)}), bf16[72,192]{1,0:T(8,128)(2,1)}) %reduce-scatter.15.cloned.1.call-update) | async-done | bytes 27664 | tf_op jit(solution)/shard_map/reduce_scatter | solution.py:286
  (224 shorter events, 187.9 us)
Async XLA Ops:
  7.2 94.4 %copy-start.7 = (bf16[1,1,2,448,576]{4,3,2,1,0:T(8,128)(2,1)S(1)}, bf16[1,1,2,448,576]{4,3,2,1,0:T(8,128)(2,1)}, u32[]{:S(2)}) copy-start(bf16[1,1,2,448,576]{4,3,2,1,0:T(8,128)(2,1)} %param.12) | copy-start | bytes 3096580
  7.2 179.7 %all-gather.5.cloned.1.call-start = ((), (), s32[]{:S(2)}) async-start(), calls=%async_computation.8 | async-start | bytes 3440640 | tf_op jit(solution)/shard_map/while/body/eval_jaxpr/all_gather | solution.py:125
  34.1 73.1 %copy-start.37 = (f32[576]{0:T(1024)}, f32[576]{0:T(1024)S(1)}, u32[]{:S(2)}) copy-start(f32[576]{0:T(1024)S(1)} %convert_element_type.223) | copy-start | bytes 6916
  36.5 70.7 %copy-start.39 = (f32[896]{0:T(1024)}, f32[896]{0:T(1024)S(1)}, u32[]{:S(2)}) copy-start(f32[896]{0:T(1024)S(1)} %rsqrt.27) | copy-start | bytes 10756
  67.5 34.4 %copy-start.30 = (bf16[576,192]{1,0:T(8,128)(2,1)}, bf16[576,192]{1,0:T(8,128)(2,1)S(1)}, u32[]{:S(2)}) copy-start(bf16[576,192]{1,0:T(8,128)(2,1)S(1)} %all_gather.43) | copy-start | bytes 663556
  101.9 80.1 %copy-start.5 = (bf16[1,1,2,448,576]{4,3,2,1,0:T(8,128)(2,1)}, bf16[1,1,2,448,576]{4,3,2,1,0:T(8,128)(2,1)S(1)}, u32[]{:S(2)}) copy-start(bf16[1,1,2,448,576]{4,3,2,1,0:T(8,128)(2,1)S(1)} %multiply_convert_fusion.3) | copy-start | bytes 3096580
  105.6 77.6 %copy-start.26 = (f32[896,32]{0,1:T(8,128)}, f32[896,32]{0,1:T(8,128)S(1)}, u32[]{:S(2)}) copy-start(f32[896,32]{0,1:T(8,128)S(1)} %get-tuple-element.105) | copy-start | bytes 344068
  108.8 226.9 %all-gather.9.cloned.1.call-start = ((), (), s32[]{:S(2)}) async-start(), calls=%async_computation.10 | async-start | bytes 1990656 | tf_op jit(solution)/shard_map/all_gather | solution.py:98
  109.6 232.8 %all-gather.7.cloned.1.call-start = ((), (), s32[]{:S(2)}) async-start(), calls=%async_computation.9 | async-start | bytes 1990656 | tf_op jit(solution)/shard_map/all_gather | solution.py:97
  110.3 238.5 %all-gather.11.cloned.1.call-start = ((), (), s32[]{:S(2)}) async-start(), calls=%async_computation.11 | async-start | bytes 2211840 | tf_op jit(solution)/shard_map/all_gather | solution.py:99
  110.9 556.9 %reduce-scatter.27.cloned.1.call-start = ((), (), s32[]{:S(2)}) async-start(), calls=%async_computation.19 | async-start | bytes 829440
  144.0 38.1 %copy-start.13 = (bf16[576,576]{1,0:T(8,128)(2,1)}, bf16[576,576]{1,0:T(8,128)(2,1)S(1)}, u32[]{:S(2)}) copy-start(bf16[576,576]{1,0:T(8,128)(2,1)S(1)} %all_gather.46) | copy-start | bytes 1990660
  183.5 41.4 %copy-start.8 = (bf16[896,9,32]{0,2,1:T(8,128)(2,1)}, bf16[896,9,32]{0,2,1:T(8,128)(2,1)S(1)}, u32[]{:S(2)}) copy-start(bf16[896,9,32]{0,2,1:T(8,128)(2,1)S(1)} %get-tuple-element.94) | copy-start | bytes 1548292
  183.5 41.4 %copy-start.10 = (bf16[896,9,32]{0,2,1:T(8,128)(2,1)}, bf16[896,9,32]{0,2,1:T(8,128)(2,1)S(1)}, u32[]{:S(2)}) copy-start(bf16[896,9,32]{0,2,1:T(8,128)(2,1)S(1)} %get-tuple-element.95) | copy-start | bytes 1548292
  188.8 36.0 %copy-start.15 = (bf16[3584,192]{0,1:T(8,128)(2,1)}, bf16[3584,192]{0,1:T(8,128)(2,1)S(1)}, u32[]{:S(2)}) copy-start(bf16[3584,192]{0,1:T(8,128)(2,1)S(1)} %get-tuple-element.91) | copy-start | bytes 4128772
  188.9 181.8 %copy-start.17 = (bf16[3584,192]{0,1:T(8,128)(2,1)}, bf16[3584,192]{0,1:T(8,128)(2,1)S(1)}, u32[]{:S(2)}) copy-start(bf16[3584,192]{0,1:T(8,128)(2,1)S(1)} %get-tuple-element.90) | copy-start | bytes 4128772
  334.1 29.8 %copy-start.3 = (f32[896,576]{0,1:T(8,128)}, f32[896,576]{0,1:T(8,128)S(1)}, u32[]{:S(2)}) copy-start(f32[896,576]{0,1:T(8,128)S(1)} %get-tuple-element.117) | copy-start | bytes 6193156
  370.5 29.0 %copy-start.22 = (bf16[896,576]{0,1:T(8,128)(2,1)}, bf16[896,576]{0,1:T(8,128)(2,1)S(1)}, u32[]{:S(2)}) copy-start(bf16[896,576]{0,1:T(8,128)(2,1)S(1)} %convolution_convert_fusion.3) | copy-start | bytes 3096580
  370.5 28.9 %copy-start.35 = (f32[3,896]{1,0:T(4,128)}, f32[3,896]{1,0:T(4,128)S(1)}, u32[]{:S(2)}) copy-start(f32[3,896]{1,0:T(4,128)S(1)} %get-tuple-element.100) | copy-start | bytes 32260
  370.6 297.2 %reduce-scatter.25.cloned.1.call-start = ((), (), s32[]{:S(2)}) async-start(), calls=%async_computation.18 | async-start | bytes 829440
  399.5 31.8 %copy-start.16 = (bf16[3584,192]{0,1:T(8,128)(2,1)S(1)}, bf16[3584,192]{0,1:T(8,128)(2,1)}, u32[]{:S(2)}) copy-start(bf16[3584,192]{0,1:T(8,128)(2,1)} %copy-done.15) | copy-start | bytes 4128772
  585.9 127.4 %reduce-scatter.23.cloned.1.call-start = ((), (), s32[]{:S(2)}) async-start(), calls=%async_computation.17 | async-start | bytes 2211840 | tf_op jit(solution)/shard_map/reduce_scatter | solution.py:304
  591.6 190.5 %reduce-scatter.19.cloned.1.call-start = ((), (), s32[]{:S(2)}) async-start(), calls=%async_computation.15 | async-start | bytes 1990656 | tf_op jit(solution)/shard_map/reduce_scatter | solution.py:298
  602.2 248.2 %reduce-scatter.21.cloned.1.call-start = ((), (), s32[]{:S(2)}) async-start(), calls=%async_computation.16 | async-start | bytes 1990656 | tf_op jit(solution)/shard_map/reduce_scatter | solution.py:301
  602.4 27.2 %slice-start = ((s8[19267584]{0:T(1024)(128)(4,1)}), s8[4194304]{0:T(1024)(128)(4,1)S(1)}, s32[]{:S(2)}) async-start(s8[19267584]{0:T(1024)(128)(4,1)} %bitcast.196), calls=%async_computation.21 | async-start | bytes 8388608
  602.5 27.2 %slice-start.1 = ((s8[19267584]{0:T(1024)(128)(4,1)}), s8[4194304]{0:T(1024)(128)(4,1)S(1)}, s32[]{:S(2)}) async-start(s8[19267584]{0:T(1024)(128)(4,1)} %bitcast.196), calls=%async_computation.22 | async-start | bytes 8388608
  602.5 27.1 %slice-start.2 = ((s8[19267584]{0:T(1024)(128)(4,1)}), s8[4194304]{0:T(1024)(128)(4,1)S(1)}, s32[]{:S(2)}) async-start(s8[19267584]{0:T(1024)(128)(4,1)} %bitcast.196), calls=%async_computation.23 | async-start | bytes 8388608
  636.5 250.9 %all-reduce.12.cloned.1.call-start = ((), (), s32[]{:S(2)}) async-start(), calls=%async_computation.20 | async-start | bytes 1744896 | tf_op jit(solution)/shard_map/psum | solution.py:310
  652.2 198.2 %copy-start.36 = (f32[3,896]{1,0:T(4,128)S(1)}, f32[3,896]{1,0:T(4,128)}, u32[]{:S(2)}) copy-start(f32[3,896]{1,0:T(4,128)} %copy-done.35) | copy-start | bytes 32260
  850.3 93.2 %reduce-scatter.13.cloned.1.call-start = ((), (), s32[]{:S(2)}) async-start(), calls=%async_computation.12 | async-start | bytes 6881280 | tf_op jit(solution)/shard_map/while/body/eval_jaxpr/reduce_scatter | solution.py:248
  865.9 140.2 %reduce-scatter.17.cloned.1.call-start = ((), (), s32[]{:S(2)}) async-start(), calls=%async_computation.14 | async-start | bytes 331776 | tf_op jit(solution)/shard_map/reduce_scatter | solution.py:289
  947.2 120.0 %reduce-scatter.15.cloned.1.call-start = ((), (), s32[]{:S(2)}) async-start(), calls=%async_computation.13 | async-start | bytes 331776 | tf_op jit(solution)/shard_map/reduce_scatter | solution.py:286
  (34 other events, 141.5 us)
Sparse Core Ops, SparseCore 0:
  108.9 23.6 all-gather.4
  134.8 49.6 all-gather.8
  186.7 45.5 all-gather.6
  234.3 46.5 all-gather.10
  370.7 57.8 reduce-scatter.26
  586.0 57.9 reduce-scatter.24
  647.4 65.8 reduce-scatter.22
  717.2 64.8 reduce-scatter.18
  785.5 64.7 reduce-scatter.20
  853.1 34.2 all-reduce.11
  890.1 53.4 reduce-scatter.12
  947.3 58.7 reduce-scatter.16
  1009.4 57.6 reduce-scatter.14
where the time goes:
time: 1090 us
  matrix products  367 us (34%)
  waiting for transfers between devices  323 us (30%)
  blocking collectives  188 us (17%)
  other arithmetic  167 us (15%)
  local copies, waits for them, and re-layouts  24.9 us (2%)
  between operations  16.6 us (2%)
    convert_element_type x3, other arithmetic, backward_seq(): score_grad = (attn_probs * (prob_grad - delta_grp)).astype(jnp.bfloat16)  94.9 us
    dot_general x3, matrix products, backward_seq(): jnp.einsum('qhd,kd->hqk', grad_grp, values_all[:, head_group], preferred_...  86.2 us
    reduce_scatter x1, waiting for transfers between devices, local(): lax.psum_scatter(gate_wgrad.astype(jnp.bfloat16), 'fsdp', scatter_dimensi...  68.8 us
    reduce_scatter x1, waiting for transfers between devices, local(): lax.psum_scatter(up_wgrad.astype(jnp.bfloat16), 'fsdp', scatter_dimension...  68.3 us
    reduce_scatter x1, waiting for transfers between devices, local(): lax.psum_scatter(key_wgrad.astype(jnp.bfloat16), 'fsdp', scatter_dimensio...  61 us
    dot_general x3, matrix products, masked_scores(): jnp.einsum('qhd,kd->hqk', query_grp, key_grp, preferred_element_type=jnp....  53.7 us
    reduce_scatter x1, waiting for transfers between devices, backward_seq(): lax.psum_scatter(kv_terms, 'ctx', scatter_dimension=0, tiled=True)  47.8 us
    dot_general x3, matrix products, backward_seq(): jnp.einsum('hqk,qhd->kd', attn_probs.astype(jnp.bfloat16), grad_grp, pref...  46.4 us
  transfers between devices with their start and end apart: 13, of which 7 were waited for; matrix products, arithmetic and copies ran while one was open for 47% of the time, Pallas kernels for 0%

commit v1 on v0

--- a/solution.py
+++ b/solution.py
@@ -1,6 +1,8 @@
 import jax
 import jax.numpy as jnp
 from jax import lax
+from jax.experimental import pallas as pl
+from jax.experimental.pallas import tpu as pltpu
 from jax.sharding import PartitionSpec as P
 
 HD = 64
@@ -35,21 +37,173 @@
     return lax.rsqrt(jnp.mean(field * field, axis=-1, keepdims=True) + NORM_EPS)
 
 
-def natural_rows(row_ids, block_len, ctx_count):
-    device_id = row_ids // (2 * block_len)
-    in_pair = row_ids // block_len % 2
-    within = row_ids % block_len
-    block_id = jnp.where(in_pair == 0, device_id, 2 * ctx_count - 1 - device_id)
-    return block_id * block_len + within
-
-
-def masked_scores(query_grp, key_grp, query_nat, key_nat):
-    scores = (
-        jnp.einsum("qhd,kd->hqk", query_grp, key_grp, preferred_element_type=jnp.float32)
-        * ATTN_SCALE
-    )
-    allowed = query_nat[:, None] >= key_nat[None, :]
-    return jnp.where(allowed[None], scores, MASKED)
+def dot_nt(left, right):
+    return lax.dot_general(
+        left, right, (((1,), (1,)), ((), ())), preferred_element_type=jnp.float32
+    )
+
+
+def dot_nn(left, right):
+    return jnp.dot(left, right, preferred_element_type=jnp.float32)
+
+
+def dealt_index(natural, block_count):
+    half = block_count // 2
+    return jnp.where(natural < half, 2 * natural, 2 * (block_count - 1 - natural) + 1)
+
+
+def attention_forward_kernel(
+    block_ref, within_ref, query_ref, key_ref, value_t_ref, out_ref, lse_ref, acc, top, total
+):
+    block_count, block_len = key_ref.shape[2], key_ref.shape[3]
+    mine = block_ref[pl.program_id(2)]
+    query = query_ref[0, 0, 0]
+
+    at = dealt_index(mine, block_count)
+    scores = dot_nt(key_ref[0, 0, at], query)
+    key_ids = lax.broadcasted_iota(jnp.int32, scores.shape, 0)
+    scores = jnp.where(key_ids <= within_ref[...], scores, MASKED)
+    row_max = jnp.max(scores, axis=0, keepdims=True)
+    exponent = jnp.exp(scores - row_max)
+    top[...] = row_max
+    total[...] = jnp.sum(exponent, axis=0, keepdims=True)
+    acc[...] = dot_nn(value_t_ref[0, 0, at], exponent.astype(jnp.bfloat16))
+
+    @pl.loop(0, mine)
+    def _(step):
+        at = dealt_index(step, block_count)
+        scores = dot_nt(key_ref[0, 0, at], query)
+        old_max = top[...]
+        row_max = jnp.maximum(old_max, jnp.max(scores, axis=0, keepdims=True))
+        exponent = jnp.exp(scores - row_max)
+        shrink = jnp.exp(old_max - row_max)
+        top[...] = row_max
+        total[...] = total[...] * shrink + jnp.sum(exponent, axis=0, keepdims=True)
+        acc[...] = acc[...] * shrink + dot_nn(
+            value_t_ref[0, 0, at], exponent.astype(jnp.bfloat16)
+        )
+
+    out_ref[0, 0, 0] = acc[...] / total[...]
+    lse_ref[0, 0, 0] = top[...] + jnp.log(total[...])
+
+
+def attention_backward_kernel(
+    block_ref,
+    within_ref,
+    query_ref,
+    grad_ref,
+    lse_ref,
+    delta_ref,
+    key_ref,
+    key_t_ref,
+    value_ref,
+    query_out,
+    key_out,
+    value_out,
+):
+    block_count, block_len = key_ref.shape[2], key_ref.shape[3]
+    mine = block_ref[pl.program_id(2)]
+    query = query_ref[0, 0, 0]
+    grad = grad_ref[0, 0, 0]
+    lse = lse_ref[0, 0, 0]
+    delta = delta_ref[0, 0, 0]
+
+    @pl.when(pl.program_id(2) == 0)
+    def _():
+        key_out[...] = jnp.zeros_like(key_out)
+        value_out[...] = jnp.zeros_like(value_out)
+
+    def one_block(natural, diagonal):
+        at = dealt_index(natural, block_count)
+        scores = dot_nt(key_ref[0, 0, at], query)
+        probs = jnp.exp(scores - lse)
+        if diagonal:
+            key_ids = lax.broadcasted_iota(jnp.int32, scores.shape, 0)
+            probs = jnp.where(key_ids <= within_ref[...], probs, 0.0)
+        prob_grad = dot_nt(value_ref[0, 0, at], grad)
+        score_grad = (probs * (prob_grad - delta)).astype(jnp.bfloat16)
+        value_out[0, 0, at] += dot_nn(probs.astype(jnp.bfloat16), grad)
+        key_out[0, 0, at] += dot_nn(score_grad, query)
+        return dot_nn(key_t_ref[0, 0, at], score_grad)
+
+    query_out[0, 0, 0] = one_block(mine, True)
+
+    @pl.loop(0, mine)
+    def _(step):
+        query_out[0, 0, 0] += one_block(step, False)
+
+
+def attention_specs(seqs, groups, rows, block_count, block_len):
+    smem = pl.BlockSpec(memory_space=pltpu.SMEM)
+    within = pl.BlockSpec((1, rows), lambda s, g, b: (0, 0))
+
+    def own(*dims):
+        return pl.BlockSpec((1, 1, 1) + dims, lambda s, g, b: (s, g, b, 0, 0))
+
+    def shared(*dims):
+        return pl.BlockSpec((1, 1, block_count) + dims, lambda s, g, b: (s, g, 0, 0, 0))
+
+    return smem, within, own, shared
+
+
+def attention_forward(blocks, within, query, key, value_t):
+    seqs, groups, pair, rows, _ = query.shape
+    block_count, block_len = key.shape[2], key.shape[3]
+    smem, within_spec, own, shared = attention_specs(seqs, groups, rows, block_count, block_len)
+    pairs = seqs * groups * pair * rows * block_len * block_count * 9 // 16
+    return pl.pallas_call(
+        attention_forward_kernel,
+        grid=(seqs, groups, pair),
+        out_shape=(
+            jax.ShapeDtypeStruct((seqs, groups, pair, HD, rows), jnp.float32),
+            jax.ShapeDtypeStruct((seqs, groups, pair, 1, rows), jnp.float32),
+        ),
+        in_specs=[smem, within_spec, own(rows, HD), shared(block_len, HD), shared(HD, block_len)],
+        out_specs=(own(HD, rows), own(1, rows)),
+        scratch_shapes=[
+            pltpu.VMEM((HD, rows), jnp.float32),
+            pltpu.VMEM((1, rows), jnp.float32),
+            pltpu.VMEM((1, rows), jnp.float32),
+        ],
+        compiler_params=pltpu.CompilerParams(vmem_limit_bytes=48 * 1024 * 1024),
+        cost_estimate=pl.CostEstimate(
+            flops=4 * HD * pairs, bytes_accessed=8 * query.size, transcendentals=pairs
+        ),
+        name="attention_forward",
+    )(blocks, within, query, key, value_t)
+
+
+def attention_backward(blocks, within, query, grad, lse, delta, key, key_t, value):
+    seqs, groups, pair, rows, _ = query.shape
+    block_count, block_len = key.shape[2], key.shape[3]
+    smem, within_spec, own, shared = attention_specs(seqs, groups, rows, block_count, block_len)
+    pairs = seqs * groups * pair * rows * block_len * block_count * 9 // 16
+    return pl.pallas_call(
+        attention_backward_kernel,
+        grid=(seqs, groups, pair),
+        out_shape=(
+            jax.ShapeDtypeStruct((seqs, groups, pair, HD, rows), jnp.float32),
+            jax.ShapeDtypeStruct((seqs, groups, block_count, block_len, HD), jnp.float32),
+            jax.ShapeDtypeStruct((seqs, groups, block_count, block_len, HD), jnp.float32),
+        ),
+        in_specs=[
+            smem,
+            within_spec,
+            own(rows, HD),
+            own(rows, HD),
+            own(1, rows),
+            own(1, rows),
+            shared(block_len, HD),
+            shared(HD, block_len),
+            shared(block_len, HD),
+        ],
+        out_specs=(own(HD, rows), shared(block_len, HD), shared(block_len, HD)),
+        compiler_params=pltpu.CompilerParams(vmem_limit_bytes=56 * 1024 * 1024),
+        cost_estimate=pl.CostEstimate(
+            flops=10 * HD * pairs, bytes_accessed=20 * query.size, transcendentals=pairs
+        ),
+        name="attention_backward",
+    )(blocks, within, query, grad, lse, delta, key, key_t, value)
 
 
 def rows_by_cols(left, right):
@@ -83,10 +237,8 @@
     ctx_id = lax.axis_index("ctx")
     layer_in = tokens.reshape(row_total, model_width).astype(jnp.float32)
     cosines, sine_vals = rope_tables(positions.reshape(row_total))
-    local_nat = natural_rows(
-        ctx_id * pair_len + jnp.arange(pair_len, dtype=jnp.int32), block_len, ctx_count
-    )
-    key_nat = natural_rows(jnp.arange(pair_len * ctx_count, dtype=jnp.int32), block_len, ctx_count)
+    block_total = 2 * ctx_count
+    own_blocks = jnp.stack([ctx_id, block_total - 1 - ctx_id]).astype(jnp.int32)
     weights_full = (
         lax.all_gather(attn_gain, "fsdp", axis=0, tiled=True),
         lax.all_gather(w_query, "fsdp", axis=0, tiled=True),
@@ -118,41 +270,29 @@
     key_value = jnp.concatenate(
         [key_rows.reshape(row_total, kv_width), value_rows], axis=-1
     ).reshape(seq_count, pair_len, 2 * kv_width)
-    query_seqs = queries.reshape(seq_count, pair_len, num_heads, HD)
-
-    def forward_seq(carried, element):
-        query_seq, kv_seq = element
-        kv_all = lax.all_gather(kv_seq, "ctx", axis=0, tiled=True)
-        keys_all = kv_all[:, :kv_width].reshape(-1, kv_heads, HD)
-        values_all = kv_all[:, kv_width:].reshape(-1, kv_heads, HD)
-        out_parts = []
-        lse_parts = []
-        for head_group in range(kv_heads):
-            head_lo = head_group * group_size
-            query_grp = query_seq[:, head_lo : head_lo + group_size]
-            scores = masked_scores(query_grp, keys_all[:, head_group], local_nat, key_nat)
-            row_max = jnp.max(scores, axis=-1, keepdims=True)
-            exponent = jnp.exp(scores - row_max)
-            row_total_exp = jnp.sum(exponent, axis=-1, keepdims=True)
-            attn_probs = (exponent / row_total_exp).astype(jnp.bfloat16)
-            out_parts.append(
-                jnp.einsum(
-                    "hqk,kd->qhd",
-                    attn_probs,
-                    values_all[:, head_group],
-                    preferred_element_type=jnp.float32,
-                )
-            )
-            lse_parts.append((row_max + jnp.log(row_total_exp))[:, :, 0])
-        attended_seq = (
-            jnp.concatenate(out_parts, axis=1).reshape(pair_len, query_width).astype(jnp.bfloat16)
+
+    def by_group(rows):
+        split = rows.reshape(seq_count, 2, block_len, kv_heads, group_size, HD)
+        return split.transpose(0, 3, 1, 4, 2, 5).reshape(
+            seq_count, kv_heads, 2, group_size * block_len, HD
         )
-        log_sum = jnp.concatenate(lse_parts, axis=0).T
-        return (carried, (attended_seq, log_sum))
-
-    forward_out = lax.scan(forward_seq, None, (query_seqs, key_value))
-    attended, log_sums = forward_out[1]
-    attended_flat = attended.reshape(row_total, query_width)
+
+    def from_group(rows_t):
+        split = rows_t.reshape(seq_count, kv_heads, 2, HD, group_size, block_len)
+        return split.transpose(0, 2, 5, 1, 4, 3).reshape(row_total, num_heads, HD)
+
+    within = jnp.tile(jnp.arange(block_len, dtype=jnp.int32), group_size)[None, :]
+    query_groups = by_group(queries * jnp.bfloat16(ATTN_SCALE))
+    kv_all = lax.all_gather(key_value, "ctx", axis=1, tiled=True).reshape(
+        seq_count, block_total, block_len, 2, kv_heads, HD
+    )
+    keys_all = kv_all[:, :, :, 0].transpose(0, 3, 1, 2, 4)
+    values_all = kv_all[:, :, :, 1].transpose(0, 3, 1, 2, 4)
+    keys_t = kv_all[:, :, :, 0].transpose(0, 3, 1, 4, 2)
+    values_t = kv_all[:, :, :, 1].transpose(0, 3, 1, 4, 2)
+    attended_t, log_sums = attention_forward(own_blocks, within, query_groups, keys_all, values_t)
+    attended = from_group(attended_t).reshape(row_total, query_width)
+    attended_flat = attended.astype(jnp.bfloat16)
     hidden = layer_in + jnp.dot(attended_flat, out_w, preferred_element_type=jnp.float32)
     inv_two = rms_scale(hidden)
     second = (hidden * inv_two * gain_two.astype(jnp.float32)).astype(jnp.bfloat16)
@@ -160,18 +300,6 @@
     up_proj = jnp.dot(second, up_w, preferred_element_type=jnp.float32)
     inner_act = (jax.nn.silu(gate_proj) * up_proj).astype(jnp.bfloat16)
     block_out = hidden + jnp.dot(inner_act, down_w, preferred_element_type=jnp.float32)
-    weights_back = (
-        lax.all_gather(attn_gain, "fsdp", axis=0, tiled=True),
-        lax.all_gather(w_query, "fsdp", axis=0, tiled=True),
-        lax.all_gather(w_key, "fsdp", axis=0, tiled=True),
-        lax.all_gather(w_value, "fsdp", axis=0, tiled=True),
-        lax.all_gather(w_out, "fsdp", axis=0, tiled=True),
-        lax.all_gather(mlp_gain, "fsdp", axis=0, tiled=True),
-        lax.all_gather(w_gate, "fsdp", axis=0, tiled=True),
-        lax.all_gather(w_up, "fsdp", axis=0, tiled=True),
-        lax.all_gather(w_down, "fsdp", axis=0, tiled=True),
-    )
-    gain_one, query_w, key_w, value_w, out_w, gain_two, gate_w, up_w, down_w = weights_back
     grad_out = cotangent.reshape(row_total, model_width)
     down_wgrad = rows_by_cols(inner_act, grad_out)
     inner_grad = times_transpose(grad_out, down_w)
@@ -192,66 +320,37 @@
     )
     hidden_low = hidden_grad.astype(jnp.bfloat16)
     out_wgrad = rows_by_cols(attended_flat, hidden_low)
-    attended_grad = (
-        times_transpose(hidden_low, out_w)
-        .astype(jnp.bfloat16)
-        .reshape(seq_count, pair_len, num_heads, HD)
-    )
-
-    def backward_seq(carried, element):
-        query_seq, kv_seq, grad_seq, lse_seq = element
-        kv_all = lax.all_gather(kv_seq, "ctx", axis=0, tiled=True)
-        keys_all = kv_all[:, :kv_width].reshape(-1, kv_heads, HD)
-        values_all = kv_all[:, kv_width:].reshape(-1, kv_heads, HD)
-        query_parts = []
-        delta_parts = []
-        key_parts = []
-        value_parts = []
-        for head_group in range(kv_heads):
-            head_lo = head_group * group_size
-            query_grp = query_seq[:, head_lo : head_lo + group_size]
-            grad_grp = grad_seq[:, head_lo : head_lo + group_size]
-            scores = masked_scores(query_grp, keys_all[:, head_group], local_nat, key_nat)
-            attn_probs = jnp.exp(scores - lse_seq[:, head_lo : head_lo + group_size].T[:, :, None])
-            prob_grad = jnp.einsum(
-                "qhd,kd->hqk",
-                grad_grp,
-                values_all[:, head_group],
-                preferred_element_type=jnp.float32,
-            )
-            delta_grp = jnp.sum(attn_probs * prob_grad, axis=-1, keepdims=True)
-            score_grad = (attn_probs * (prob_grad - delta_grp)).astype(jnp.bfloat16)
-            query_parts.append(
-                jnp.einsum(
-                    "hqk,kd->qhd",
-                    score_grad,
-                    keys_all[:, head_group],
-                    preferred_element_type=jnp.float32,
-                )
-                * ATTN_SCALE
-            )
-            delta_parts.append(delta_grp[:, :, 0])
-            key_parts.append(
-                jnp.einsum("hqk,qhd->kd", score_grad, query_grp, preferred_element_type=jnp.float32)
-                * ATTN_SCALE
-            )
-            value_parts.append(
-                jnp.einsum(
-                    "hqk,qhd->kd",
-                    attn_probs.astype(jnp.bfloat16),
-                    grad_grp,
-                    preferred_element_type=jnp.float32,
-                )
-            )
-        query_grad_seq = jnp.concatenate(query_parts, axis=1)
-        kv_terms = jnp.concatenate(key_parts + value_parts, axis=-1)
-        kv_grad_seq = lax.psum_scatter(kv_terms, "ctx", scatter_dimension=0, tiled=True)
-        return (carried, (query_grad_seq, kv_grad_seq))
-
-    backward_out = lax.scan(backward_seq, None, (query_seqs, key_value, attended_grad, log_sums))
-    query_grad_all, kv_grad_all = backward_out[1]
+    attended_grad = times_transpose(hidden_low, out_w).astype(jnp.bfloat16)
+    delta = jnp.sum(
+        (attended * attended_grad.astype(jnp.float32)).reshape(row_total, num_heads, HD), axis=-1
+    )
+    delta_groups = (
+        delta.reshape(seq_count, 2, block_len, kv_heads, group_size)
+        .transpose(0, 3, 1, 4, 2)
+        .reshape(seq_count, kv_heads, 2, 1, group_size * block_len)
+    )
+    query_grad_t, key_terms, value_terms = attention_backward(
+        own_blocks,
+        within,
+        query_groups,
+        by_group(attended_grad),
+        log_sums,
+        delta_groups,
+        keys_all,
+        keys_t,
+        values_all,
+    )
+    kv_terms = (
+        jnp.stack([key_terms, value_terms], axis=1)
+        .transpose(0, 3, 4, 1, 2, 5)
+        .reshape(seq_count, block_total * block_len, 2 * kv_width)
+    )
+    kv_grad_all = lax.psum_scatter(
+        kv_terms.astype(jnp.bfloat16), "ctx", scatter_dimension=1, tiled=True
+    ).astype(jnp.float32)
+    query_grad_all = from_group(query_grad_t) * ATTN_SCALE
     query_back = (
-        rotate(query_grad_all.reshape(row_total, num_heads, HD), cosines, -sine_vals)
+        rotate(query_grad_all, cosines, -sine_vals)
         .reshape(row_total, query_width)
         .astype(jnp.bfloat16)
     )

time: 1090 us -> 964 us (0.88)
  matrix products: 367 us -> 78.7 us
  other arithmetic: 167 us -> 42.8 us
  local copies, waits for them, and re-layouts: 24.9 us -> 132 us
  waiting for transfers between devices: 323 us -> 412 us
  Pallas kernels: 0 us -> 86.9 us
    dot_general x18 -> x0, matrix products: 293 us -> none  [the longest x3 86.2 us: backward_seq(): jnp.einsum('qhd,kd->hqk', grad_grp, values_all[:, head_group], preferred_...]
    unnamed x15 -> x16, waiting for transfers between devices: 2.07 us -> 118 us
    convert_element_type x4 -> x2, other arithmetic: 95 us -> 3.81 us  [the longest x1 3.66 us: local(): kv_terms.astype(jnp.bfloat16)]
    pallas_call x0 -> x2, Pallas kernels: none -> 86.9 us  [the longest x1 52.8 us: attention_backward(): pl.pallas_call(attention_backward_kernel, grid=(seqs, groups, pair), out_...]
    reduce_scatter x1 -> x0, waiting for transfers between devices: 47.8 us -> none  [backward_seq(): lax.psum_scatter(kv_terms, 'ctx', scatter_dimension=0, tiled=True)]
    reduce_sum x3 -> x1, other arithmetic: 45.3 us -> 1.74 us  [local(): jnp.sum((attended * attended_grad.astype(jnp.float32)).reshape(row_total,...]
    reduce_scatter x1, waiting for transfers between devices: 18.9 us -> 61.1 us  [local(): lax.psum_scatter(value_wgrad.astype(jnp.bfloat16), 'fsdp', scatter_dimens...]
    reduce_scatter x1, waiting for transfers between devices: 61 us -> 25 us  [local(): lax.psum_scatter(key_wgrad.astype(jnp.bfloat16), 'fsdp', scatter_dimensio...]
  transfers between devices with their start and end apart: 13 -> 13, of which waited for: 7 -> 8; matrix products, arithmetic and copies ran while one was open for 47% -> 17% of each run, Pallas kernels for 0% -> 4%
where the time goes in v1:
time: 964 us; the launch traced here: 955 us
  waiting for transfers between devices  412 us (43%)
  blocking collectives  185 us (19%)
  local copies, waits for them, and re-layouts  132 us (14%)
  Pallas kernels  86.9 us (9%)
  matrix products  78.7 us (8%)
  other arithmetic  42.8 us (4%)
  between operations  16.2 us (2%)
    unnamed x16, waiting for transfers between devices  118 us
    reduce_scatter x1, waiting for transfers between devices, local(): lax.psum_scatter(down_wgrad.astype(jnp.bfloat16), 'fsdp', scatter_dimensi...  69.5 us
    reduce_scatter x1, waiting for transfers between devices, local(): lax.psum_scatter(gate_wgrad.astype(jnp.bfloat16), 'fsdp', scatter_dimensi...  69.3 us
    reduce_scatter x1, waiting for transfers between devices, local(): lax.psum_scatter(up_wgrad.astype(jnp.bfloat16), 'fsdp', scatter_dimension...  69 us
    reduce_scatter x1, waiting for transfers between devices, local(): lax.psum_scatter(value_wgrad.astype(jnp.bfloat16), 'fsdp', scatter_dimens...  61.1 us
    pallas_call x1, Pallas kernels, attention_backward(): pl.pallas_call(attention_backward_kernel, grid=(seqs, groups, pair), out_...  52.8 us
    unnamed x2, blocking collectives  45 us
    unnamed x93, local copies, waits for them, and re-layouts  41.7 us
  transfers between devices with their start and end apart: 13, of which 8 were waited for; matrix products, arithmetic and copies ran while one was open for 17% of the time, Pallas kernels for 4%

profile of v1, /device:TPU:0, one launch (start us, length us, event | category | flops | bytes accessed | tf_op | source)
XLA Modules:
  0.0 954.5 jit_solution(2212749760824354740)
XLA Ops:
  12.8 23.7 %all-reduce.7 = (bf16[576]{0:T(1024)(128)(2,1)S(1)}, bf16[576]{0:T(1024)(128)(2,1)}) all-reduce(bf16[576]{0:T(1024)(128)(2,1)S(1)} %dynamic-update-slice, bf16[576]{0:T(1024)(128)(2,1)S(1)} %dynamic-update-slice.1), channel_id=1, replica_groups=mesh['ctx'=4,'fsdp'=8] {'fsdp'}, use_global_device_ids=true, to_apply=%add | all-reduce | flops 1152 | bytes 4608
  38.0 30.8 %all_gather.33 = bf16[576,192]{1,0:T(8,128)(2,1)S(1)} all-gather(bf16[72,192]{1,0:T(8,128)(2,1)S(1)} %copy-done.29), channel_id=1, replica_groups=mesh['ctx'=4,'fsdp'=8] {'fsdp'}, dimensions={0}, use_global_device_ids=true | all-gather | bytes 248832 | tf_op jit(solution)/shard_map/all_gather | solution.py:246
  68.8 30.9 %all_gather.32 = bf16[576,192]{1,0:T(8,128)(2,1)S(1)} all-gather(bf16[72,192]{1,0:T(8,128)(2,1)S(1)} %copy-done.30), channel_id=1, replica_groups=mesh['ctx'=4,'fsdp'=8] {'fsdp'}, dimensions={0}, use_global_device_ids=true | all-gather | bytes 248832 | tf_op jit(solution)/shard_map/all_gather | solution.py:245
  106.1 31.6 %all_gather.31 = bf16[576,576]{1,0:T(8,128)(2,1)S(1)} all-gather(bf16[72,576]{1,0:T(8,128)(2,1)S(1)} %copy-done.26), channel_id=1, replica_groups=mesh['ctx'=4,'fsdp'=8] {'fsdp'}, dimensions={0}, use_global_device_ids=true | all-gather | bytes 746496 | tf_op jit(solution)/shard_map/all_gather | solution.py:244
  158.2 35.0 %all_gather.35 = bf16[576,576]{1,0:T(8,128)(2,1)} all-gather(bf16[72,576]{1,0:T(8,128)(2,1)S(1)} %copy-done.27), channel_id=1, replica_groups=mesh['ctx'=4,'fsdp'=8] {'fsdp'}, dimensions={0}, use_global_device_ids=true | all-gather | bytes 746496 | tf_op jit(solution)/shard_map/all_gather | solution.py:247
  193.2 6.6 reshape.344
  218.0 34.2 %attention_forward.1 = (f32[1,3,2,64,1344]{4,3,2,1,0:T(8,128)S(1)}, f32[1,3,2,1,1344]{4,3,2,1,0:T(1,128)S(1)}) custom-call(s32[2]{0:T(128)S(1)} %pad_add_fusion.block_ref, s32[1,1344]{1,0:T(1,128)S(1)} %broadcast_in_dim_tile.5.within_ref, bf16[1,3,2,1344,64]{4,3,2,1,0:T(8,128)(2,1)S(1)} %bitcast.119, bf16[1,3,8,448,64]{4,3,2,1,0:T(8,128)(2,1)} %copy.72.key_ref, ...), custom_call_target="tpu_custom_call" | custom-call | flops 4161798144 | bytes 4128768 | tf_op jit(solution)/shard_map/attention_forward/pallas_call | solution.py:154
  256.1 5.1 copy.74
  271.4 6.6 fusion.16
  278.0 6.6 fusion.17
  284.5 9.5 multiply_convert_fusion
  317.8 52.8 %attention_backward.1 = (f32[1,3,2,64,1344]{4,3,2,1,0:T(8,128)}, f32[1,3,8,448,64]{4,3,2,1,0:T(8,128)}, f32[1,3,8,448,64]{4,3,2,1,0:T(8,128)}) custom-call(s32[2]{0:T(128)} %copy-done.3, s32[1,1344]{1,0:T(1,128)} %copy-done.2, bf16[1,3,2,1344,64]{4,3,2,1,0:T(8,128)(2,1)} %bitcast.118, bf16[1,3,2,1344,64]{4,3,2,1,0:T(8,128)(2,1)} %bitcast.143, ...), custom_call_target="tpu_custom_call" | custom-call | flops 10404495360 | bytes 10321920 | tf_op jit(solution)/shard_map/attention_backward/pallas_call | solution.py:181
  378.6 5.1 copy.82
  397.3 5.3 convolution_convert_fusion.2
  402.7 5.4 convolution_convert_fusion.1
  408.2 6.0 convolution_convert_fusion
  414.2 36.7 %reduce-scatter.27.cloned.1.call-done = bf16[72,576]{1,0:T(8,128)(2,1)} async-done(((bf16[576,576]{1,0:T(8,128)(2,1)}), bf16[72,576]{1,0:T(8,128)(2,1)}) %reduce-scatter.27.cloned.1.call-update) | async-done | bytes 82960
  450.9 62.7 %reduce-scatter.29.cloned.1.call-done = bf16[72,576]{1,0:T(8,128)(2,1)} async-done(((bf16[576,576]{1,0:T(8,128)(2,1)}), bf16[72,576]{1,0:T(8,128)(2,1)}) %reduce-scatter.29.cloned.1.call-update) | async-done | bytes 82960
  513.7 69.3 %reduce-scatter.19.cloned.1.call-done = bf16[72,1536]{1,0:T(8,128)(2,1)} async-done(((bf16[576,1536]{1,0:T(8,128)(2,1)}), bf16[72,1536]{1,0:T(8,128)(2,1)}) %reduce-scatter.19.cloned.1.call-update) | async-done | bytes 221200 | tf_op jit(solution)/shard_map/reduce_scatter | solution.py:397
  583.0 69.0 %reduce-scatter.21.cloned.1.call-done = bf16[72,1536]{1,0:T(8,128)(2,1)} async-done(((bf16[576,1536]{1,0:T(8,128)(2,1)}), bf16[72,1536]{1,0:T(8,128)(2,1)}) %reduce-scatter.21.cloned.1.call-update) | async-done | bytes 221200 | tf_op jit(solution)/shard_map/reduce_scatter | solution.py:400
  652.0 69.5 %reduce-scatter.23.cloned.1.call-done = bf16[192,576]{1,0:T(8,128)(2,1)} async-done(((bf16[1536,576]{1,0:T(8,128)(2,1)}), bf16[192,576]{1,0:T(8,128)(2,1)}) %reduce-scatter.23.cloned.1.call-update) | async-done | bytes 221200 | tf_op jit(solution)/shard_map/reduce_scatter | solution.py:403
  721.6 5.1 convert_bitcast_fusion
  730.4 7.7 copy.83
  738.1 6.3 convert_element_type.234
  744.4 12.6 %copy.92 = bf16[1,3584,384]{2,0,1:T(2,128)(2,1)} copy(bf16[1,3584,384]{1,2,0:T(8,128)(2,1)} %convert_element_type.234) | data formatting | bytes 5505024
  762.6 6.4 convolution_add_fusion.1
  780.7 16.5 %reduce-scatter.25.cloned.1.call-done = bf16[896,384]{1,0:T(8,128)(2,1)} async-done(((bf16[3584,384]{1,0:T(8,128)(2,1)}), bf16[896,384]{1,0:T(8,128)(2,1)}) %reduce-scatter.25.cloned.1.call-update) | async-done | bytes 688144
  813.9 5.3 multiply_reduce_fusion.2
  826.2 21.3 %all-reduce.6 = (bf16[576]{0:T(1024)(128)(2,1)S(1)}, bf16[576]{0:T(1024)(128)(2,1)S(1)}) all-reduce(bf16[576]{0:T(1024)(128)(2,1)S(1)} %get-tuple-element.34, bf16[576]{0:T(1024)(128)(2,1)S(1)} %get-tuple-element.32), channel_id=4, replica_groups=mesh['ctx'=4,'fsdp'=8] {'fsdp'}, use_global_device_ids=true, to_apply=%region_7.8.clone | all-reduce | flops 1152 | bytes 4608
  847.7 25.0 %reduce-scatter.15.cloned.1.call-done = bf16[72,192]{1,0:T(8,128)(2,1)} async-done(((bf16[576,192]{1,0:T(8,128)(2,1)}), bf16[72,192]{1,0:T(8,128)(2,1)}) %reduce-scatter.15.cloned.1.call-update) | async-done | bytes 27664 | tf_op jit(solution)/shard_map/reduce_scatter | solution.py:385
  872.7 61.1 %reduce-scatter.17.cloned.1.call-done = bf16[72,192]{1,0:T(8,128)(2,1)} async-done(((bf16[576,192]{1,0:T(8,128)(2,1)}), bf16[72,192]{1,0:T(8,128)(2,1)}) %reduce-scatter.17.cloned.1.call-update) | async-done | bytes 27664 | tf_op jit(solution)/shard_map/reduce_scatter | solution.py:388
  933.8 11.4 %all-reduce.8 = (bf16[72]{0:T(256)(128)(2,1)S(1)}, bf16[72,192]{1,0:T(8,128)(2,1)S(1)}, bf16[72,192]{1,0:T(8,128)(2,1)S(1)}, bf16[72]{0:T(256)(128)(2,1)S(1)}) all-reduce(bf16[72]{0:T(256)(128)(2,1)S(1)} %dynamic-slice.3, bf16[72,192]{1,0:T(8,128)(2,1)} %reduce-scatter.15.cloned.1.call-done, ...), channel_id=1, replica_groups=mesh['ctx'=4,'fsdp'=8] {'ctx'}, use_global_device_ids=true, to_apply=%region_8.9 | all-reduce | flops 27792 | bytes 111168 | tf_op jit(solution)/shard_map/psum | solution.py:408
  (200 shorter events, 157.2 us)
Async XLA Ops:
  7.2 186.0 %all-gather.12.cloned.1.call-start = ((), (), s32[]{:S(2)}) async-start(), calls=%async_computation.16 | async-start | bytes 3440640 | tf_op jit(solution)/shard_map/all_gather | solution.py:286
  7.3 3.7 copy-start.33
  7.3 5.0 copy-start.36
  7.3 5.3 copy-start.37
  7.3 29.3 %copy-start.11 = (bf16[1,1,2,448,576]{4,3,2,1,0:T(8,128)(2,1)S(1)}, bf16[1,1,2,448,576]{4,3,2,1,0:T(8,128)(2,1)}, u32[]{:S(2)}) copy-start(bf16[1,1,2,448,576]{4,3,2,1,0:T(8,128)(2,1)} %param.12) | copy-start | bytes 3096580
  9.0 28.9 %copy-start.31 = (s32[1,1,2,448]{3,2,1,0:T(2,128)S(1)}, s32[1,1,2,448]{3,2,1,0:T(2,128)}, u32[]{:S(2)}) copy-start(s32[1,1,2,448]{3,2,1,0:T(2,128)} %param.13) | copy-start | bytes 10756
  9.0 29.0 %copy-start.29 = (bf16[72,192]{1,0:T(8,128)(2,1)S(1)}, bf16[72,192]{1,0:T(8,128)(2,1)}, u32[]{:S(2)}) copy-start(bf16[72,192]{1,0:T(8,128)(2,1)} %param.17) | copy-start | bytes 82948
  10.9 91.5 %copy-start.5 = (f32[896,576]{0,1:T(8,128)}, f32[896,576]{0,1:T(8,128)S(1)}, u32[]{:S(2)}) copy-start(f32[896,576]{0,1:T(8,128)S(1)} %copy.75) | copy-start | bytes 6193156
  10.9 57.9 %copy-start.30 = (bf16[72,192]{1,0:T(8,128)(2,1)S(1)}, bf16[72,192]{1,0:T(8,128)(2,1)}, u32[]{:S(2)}) copy-start(bf16[72,192]{1,0:T(8,128)(2,1)} %param.16) | copy-start | bytes 82948
  36.6 65.8 %copy-start.24 = (f32[896]{0:T(1024)}, f32[896]{0:T(1024)S(1)}, u32[]{:S(2)}) copy-start(f32[896]{0:T(1024)S(1)} %rsqrt.27) | copy-start | bytes 10756
  68.8 33.6 %copy-start.21 = (bf16[576,192]{1,0:T(8,128)(2,1)}, bf16[576,192]{1,0:T(8,128)(2,1)S(1)}, u32[]{:S(2)}) copy-start(bf16[576,192]{1,0:T(8,128)(2,1)S(1)} %all_gather.33) | copy-start | bytes 663556
  103.9 34.3 %copy-start.12 = (bf16[1,1,2,448,576]{4,3,2,1,0:T(8,128)(2,1)S(1)}, bf16[1,1,2,448,576]{4,3,2,1,0:T(8,128)(2,1)}, u32[]{:S(2)}) copy-start(bf16[1,1,2,448,576]{4,3,2,1,0:T(8,128)(2,1)} %multiply_convert_fusion.3) | copy-start | bytes 3096580
  103.9 167.5 %all-gather.6.cloned.1.call-start = ((), (), s32[]{:S(2)}) async-start(), calls=%async_computation.8 | async-start | bytes 1990656 | tf_op jit(solution)/shard_map/all_gather | solution.py:249
  104.7 173.3 %all-gather.8.cloned.1.call-start = ((), (), s32[]{:S(2)}) async-start(), calls=%async_computation.9 | async-start | bytes 1990656 | tf_op jit(solution)/shard_map/all_gather | solution.py:250
  105.4 179.1 %all-gather.10.cloned.1.call-start = ((), (), s32[]{:S(2)}) async-start(), calls=%async_computation.10 | async-start | bytes 2211840 | tf_op jit(solution)/shard_map/all_gather | solution.py:251
  106.0 344.9 %reduce-scatter.27.cloned.1.call-start = ((), (), s32[]{:S(2)}) async-start(), calls=%async_computation.18 | async-start | bytes 829440
  106.1 108.9 %copy-start.2 = (s32[1,1344]{1,0:T(1,128)}, s32[1,1344]{1,0:T(1,128)S(1)}, u32[]{:S(2)}) copy-start(s32[1,1344]{1,0:T(1,128)S(1)} %broadcast_in_dim_tile.5.within_ref) | copy-start | bytes 16132
  144.3 6.7 copy-start.32
  154.0 61.1 %copy-start.3 = (s32[2]{0:T(128)}, s32[2]{0:T(128)S(1)}, u32[]{:S(2)}) copy-start(s32[2]{0:T(128)S(1)} %pad_add_fusion.block_ref) | copy-start | bytes 28
  154.0 4.2 copy-start.27
  261.3 4.7 copy-start.6
  266.0 4.2 copy-start.28
  284.5 9.5 copy-start.34
  294.0 4.1 copy-start.35
  392.8 120.9 %reduce-scatter.29.cloned.1.call-start = ((), (), s32[]{:S(2)}) async-start(), calls=%async_computation.19 | async-start | bytes 829440
  397.0 186.0 %reduce-scatter.19.cloned.1.call-start = ((), (), s32[]{:S(2)}) async-start(), calls=%async_computation.13 | async-start | bytes 1990656 | tf_op jit(solution)/shard_map/reduce_scatter | solution.py:397
  402.6 249.4 %reduce-scatter.21.cloned.1.call-start = ((), (), s32[]{:S(2)}) async-start(), calls=%async_computation.14 | async-start | bytes 1990656 | tf_op jit(solution)/shard_map/reduce_scatter | solution.py:400
  408.1 313.4 %reduce-scatter.23.cloned.1.call-start = ((), (), s32[]{:S(2)}) async-start(), calls=%async_computation.15 | async-start | bytes 2211840 | tf_op jit(solution)/shard_map/reduce_scatter | solution.py:403
  414.2 358.1 %all-reduce.12.cloned.1.call-start = ((), (), s32[]{:S(2)}) async-start(), calls=%async_computation.20 | async-start | bytes 1744896 | tf_op jit(solution)/shard_map/psum | solution.py:409
  721.5 75.6 %reduce-scatter.25.cloned.1.call-start = ((), (), s32[]{:S(2)}) async-start(), calls=%async_computation.17 | async-start | bytes 3440640
  761.7 111.1 %reduce-scatter.15.cloned.1.call-start = ((), (), s32[]{:S(2)}) async-start(), calls=%async_computation.11 | async-start | bytes 331776 | tf_op jit(solution)/shard_map/reduce_scatter | solution.py:385
  813.8 120.0 %reduce-scatter.17.cloned.1.call-start = ((), (), s32[]{:S(2)}) async-start(), calls=%async_computation.12 | async-start | bytes 331776 | tf_op jit(solution)/shard_map/reduce_scatter | solution.py:388
  (21 other events, 39.7 us)
Sparse Core Ops, SparseCore 0:
  104.0 23.5 all-gather.11
  129.8 51.3 all-gather.5
  183.4 44.5 all-gather.7
  229.9 46.5 all-gather.9
  392.9 57.9 reduce-scatter.26
  454.1 59.4 reduce-scatter.28
  517.7 65.2 reduce-scatter.18
  586.8 65.1 reduce-scatter.20
  656.1 65.4 reduce-scatter.22
  724.3 34.2 all-reduce.11
  761.8 35.3 reduce-scatter.24
  814.0 58.7 reduce-scatter.14
  876.0 57.7 reduce-scatter.16
